TPU v7x, 32 devices: a whole 2x2x4 slice. The times are simulated.
32 devices in a mesh: dp: 8 (over y, x, core), expert: 4 (over z).
Axes of the slice: x: 2, y: 2, z: 4, core: 2. Of those that a mesh axis runs over, the one named last changes fastest.
Arguments:
- residual: bfloat16 [4096, 2048], P(('dp', 'expert')), may hold values from -6 to 6
- grad_stream: bfloat16 [4096, 2048], P(('dp', 'expert')), may hold values from -6 to 6
- expert_gain: float32 [2048], replicated, may hold values from 0.5 to 1.5
- router_weight: bfloat16 [2048, 32], replicated, may hold values from -0.125 to 0.125
- gate_up_weight: bfloat16 [32, 2048, 1536], P('expert', 'dp'), may hold values from -0.125 to 0.125
- down_weight: bfloat16 [32, 2048, 768], P('expert', 'dp'), may hold values from -0.21875 to 0.21875
- need_lists: int32 [4, 2], replicated, may hold values from 0 to 31, as said below
- routes: int32 [4096, 1], P(('dp', 'expert')), may hold values from 0 to 1
Outputs:
- stream: bfloat16 [4096, 2048], P(('dp', 'expert'))
- grad_residual: bfloat16 [4096, 2048], P(('dp', 'expert'))
Inputs may be any that keep to these rules, and one draw needn't show every extreme that they name: `need_lists`: row c lists 2 experts with different owner indices (expert id // 8).
All inputs are finite; a program needn't handle non-finite values.
Results may differ from a plain program's by a relative error of at most 0.008.
Values may be sent and summed in bfloat16 or wider, within the bound.
A program may use at most 128 MiB of HBM per device.

v0:
```python
import jax
import jax.numpy as jnp
from jax import lax
from jax.sharding import PartitionSpec as P

eps = 1e-05


def partner(value, axis, stride):
    mask = 2**stride
    pairs = [(source, source ^ mask) for source in range(lax.axis_size(axis))]
    return lax.ppermute(value, axis, pairs)


def norm_factor(values):
    return lax.rsqrt(jnp.mean(values * values, axis=-1, keepdims=True) + eps)


def norm_backward(values, factor, gain, grad):
    scaled = gain * grad
    return factor * scaled - values * factor**3 * jnp.mean(values * scaled, axis=-1, keepdims=True)


def body(
    residual,
    grad_stream,
    expert_gain,
    router_weight,
    gate_up_weight,
    down_weight,
    need_lists,
    routes,
):
    column = lax.axis_index("expert")
    ranks = lax.axis_size("dp")
    parity = lax.axis_index("dp") % 2
    held = gate_up_weight.shape[0]
    width = down_weight.shape[2]
    tokens = residual.shape[0]
    listed = lax.dynamic_index_in_dim(need_lists, column, 0, keepdims=False)
    owner_of = need_lists // held
    local_of = need_lists % held
    mine = owner_of == column
    has_one = jnp.any(mine, axis=1)
    local_pick = jnp.sum(jnp.where(mine, local_of, 0), axis=1)
    owned = jnp.stack(
        [gate_up_weight[:, :, :width], gate_up_weight[:, :, width:], down_weight], axis=2
    )
    outgoing = jnp.where(
        has_one[:, None, None, None],
        jnp.take(owned, local_pick, axis=0),
        jnp.zeros((), jnp.bfloat16),
    )
    arrived = lax.all_to_all(outgoing, "expert", split_axis=0, concat_axis=0, tiled=True)
    slot_rows = jnp.take(arrived, listed // held, axis=0)
    spread_out = jnp.broadcast_to(slot_rows[None], (ranks // 2,) + slot_rows.shape).reshape(
        (ranks,) + slot_rows.shape[1:]
    )
    stream_in = residual.astype(jnp.float32)
    factor_in = norm_factor(stream_in)
    normed = (stream_in * factor_in * expert_gain).astype(jnp.bfloat16)
    router_cols = jnp.take(router_weight, listed, axis=1)
    logits = jnp.dot(normed, router_cols, preferred_element_type=jnp.float32)
    gates = jax.nn.sigmoid(logits - logits[:, ::-1])
    select = (routes == jnp.arange(2, dtype=jnp.int32)[None, :]).astype(jnp.float32)
    mix = gates * select
    mix_here = lax.dynamic_index_in_dim(mix, parity, 1, keepdims=False)
    mix_there = lax.dynamic_index_in_dim(mix, 1 - parity, 1, keepdims=False)
    grad_out = grad_stream.astype(jnp.float32)
    send_grad = (mix_there[:, None] * grad_out).astype(jnp.bfloat16)
    partner_normed, partner_grad = partner((normed, send_grad), "dp", 0)
    pair_normed = jnp.concatenate([normed, partner_normed], axis=0)
    weights = lax.all_to_all(spread_out, "dp", split_axis=0, concat_axis=1, tiled=True)[0]
    hidden = jnp.einsum(
        "td,dkf->tkf", pair_normed, weights[:, :2], preferred_element_type=jnp.float32
    )
    gate_part = hidden[:, 0]
    up_part = hidden[:, 1]
    sigma = jax.nn.sigmoid(gate_part)
    silu_gate = gate_part * sigma
    act = (silu_gate * up_part).astype(jnp.bfloat16)
    branch = jnp.einsum("tf,df->td", act, weights[:, 2], preferred_element_type=jnp.float32).astype(
        jnp.bfloat16
    )
    other_branch = partner(branch[tokens:], "dp", 0)
    branch_here = branch[:tokens].astype(jnp.float32)
    branch_there = other_branch.astype(jnp.float32)
    stream = (
        stream_in + mix_here[:, None] * branch_here + mix_there[:, None] * branch_there
    ).astype(jnp.bfloat16)
    mix_grad_here = jnp.sum(branch_here * grad_out, axis=-1)
    mix_grad_there = jnp.sum(branch_there * grad_out, axis=-1)
    grad_mix = jnp.where(
        parity == 0,
        jnp.stack([mix_grad_here, mix_grad_there], axis=1),
        jnp.stack([mix_grad_there, mix_grad_here], axis=1),
    )
    grad_branch = jnp.concatenate(
        [(mix_here[:, None] * grad_out).astype(jnp.bfloat16), partner_grad], axis=0
    )
    grad_act = jnp.einsum(
        "td,df->tf", grad_branch, weights[:, 2], preferred_element_type=jnp.float32
    )
    slope = sigma * (1.0 + gate_part * (1.0 - sigma))
    grad_hidden = jnp.stack([grad_act * up_part * slope, grad_act * silu_gate], axis=1).astype(
        jnp.bfloat16
    )
    expert_term = jnp.einsum(
        "tkf,dkf->td", grad_hidden, weights[:, :2], preferred_element_type=jnp.float32
    ).astype(jnp.bfloat16)
    other_term = partner(expert_term[tokens:], "dp", 0)
    grad_gates = grad_mix * select
    grad_logits = (
        gates * (grad_gates - jnp.sum(gates * grad_gates, axis=-1, keepdims=True))
    ).astype(jnp.bfloat16)
    grad_normed = expert_term[:tokens].astype(jnp.float32) + other_term.astype(jnp.float32)
    grad_normed = grad_normed + jnp.einsum(
        "tn,dn->td", grad_logits, router_cols, preferred_element_type=jnp.float32
    )
    grad_residual = (
        grad_out + norm_backward(stream_in, factor_in, expert_gain, grad_normed)
    ).astype(jnp.bfloat16)
    return (stream, grad_residual)


def solution(mesh):
    return jax.shard_map(
        body,
        mesh=mesh,
        in_specs=(
            P(("dp", "expert"), None),
            P(("dp", "expert"), None),
            P(),
            P(),
            P("expert", "dp", None),
            P("expert", "dp", None),
            P(),
            P(("dp", "expert"), None),
        ),
        out_specs=(P(("dp", "expert"), None), P(("dp", "expert"), None)),
        check_vma=False,
    )
```

profile of v0, /device:TPU:0, one launch (start us, length us, event | category | flops | bytes accessed | tf_op | source)
XLA Modules:
  0.0 289.3 jit_solution(1580183164395549183)
XLA Ops:
  0.6 0.0 copy-start
  0.6 0.7 fusion.64
  1.4 0.7 fusion.49
  2.1 5.0 %slice_bitcast_fusion.2 = (bf16[8,256,1,768]{3,1,0,2:T(8,128)(2,1)S(1)}, bf16[8,256,1,768]{3,1,0,2:T(8,128)(2,1)}) fusion(bf16[8,256,1536]{2,1,0:T(8,128)(2,1)} %param.12), kind=kLoop, calls=%fused_computation.11 | loop fusion | bytes 12582912 | tf_op jit(solution)/shard_map/stack | solution.py:46
  7.1 7.0 %pad_maximum_fusion = bf16[8,256,3,768]{3,1,0,2:T(8,128)(2,1)} fusion(bf16[8,256,1,768]{3,1,0,2:T(8,128)(2,1)} %bitcast.97, bf16[8,256,1,768]{3,1,0,2:T(8,128)(2,1)} %get-tuple-element.9, bf16[8,256,1,768]{3,1,0,2:T(8,128)(2,1)S(1)} %get-tuple-element.8), kind=kLoop, calls=%fused_computation.3 | loop fusion | flops 9437184 | bytes 18874368 | tf_op jit(solution)/shard_map/stack | solution.py:46
  14.1 6.8 %gather_fusion.1 = bf16[4,256,3,768]{3,1,2,0:T(8,128)(2,1)} fusion(bf16[8,256,3,768]{3,1,0,2:T(8,128)(2,1)} %pad_maximum_fusion, s32[1024]{0:T(1024)S(1)} %pad_clamp_fusion.1), kind=kCustom, calls=%fused_computation.1 | custom fusion | bytes 9437200 | tf_op jit(solution)/shard_map/jit(_take)/gather | solution.py:51
  20.8 5.2 %select_select_fusion = bf16[4,256,3,768]{3,1,2,0:T(8,128)(2,1)} fusion(bf16[4,256,3,768]{3,1,2,0:T(8,128)(2,1)} %gather_fusion.1, pred[4]{0:T(512)(128)(4,1)S(1)} %compare_and_fusion, pred[4]{0:T(512)(128)(4,1)S(1)} %get-tuple-element.6), kind=kLoop, calls=%fused_computation.8 | loop fusion | flops 4718592 | bytes 9437192 | tf_op jit(solution)/shard_map/jit(_where)/select_n | solution.py:49
  26.0 0.0 copy-start.5
  26.0 6.4 %all-to-all-start = ((bf16[4,256,3,768]{3,1,2,0:T(8,128)(2,1)}), bf16[4,256,3,768]{3,1,2,0:T(8,128)(2,1)}, u32[]{:S(2)}, u32[]{:S(2)}) async-start(bf16[4,256,3,768]{3,1,2,0:T(8,128)(2,1)} %select_select_fusion), calls=%async_computation | async-start | bytes 9437184 | tf_op jit(solution)/shard_map/all_to_all | solution.py:54
  32.5 0.0 copy-done.5
  32.5 0.2 dynamic-slice_reduce_fusion
  32.7 104.5 %all-to-all-done = bf16[4,256,3,768]{3,1,2,0:T(8,128)(2,1)} async-done(((bf16[4,256,3,768]{3,1,2,0:T(8,128)(2,1)}), bf16[4,256,3,768]{3,1,2,0:T(8,128)(2,1)}, u32[]{:S(2)}, u32[]{:S(2)}) %all-to-all-start) | async-done | bytes 4718624 | tf_op jit(solution)/shard_map/all_to_all | solution.py:54
  137.2 3.0 %gather_fusion.2 = bf16[2,256,3,768]{3,1,2,0:T(8,128)(2,1)S(1)} fusion(bf16[4,256,3,768]{3,1,2,0:T(8,128)(2,1)} %all-to-all-done, s32[1024]{0:T(1024)S(1)} %pad_clamp_fusion), kind=kCustom, calls=%fused_computation.2 | custom fusion | bytes 4718600 | tf_op jit(solution)/shard_map/jit(_take)/gather | solution.py:55
  140.3 0.3 broadcast_select_fusion
  140.6 4.7 %broadcast_in_dim.69 = bf16[4,2,256,3,768]{4,2,3,1,0:T(8,128)(2,1)} broadcast(bf16[2,256,3,768]{3,1,2,0:T(8,128)(2,1)S(1)} %broadcast_select_fusion), dimensions={1,2,3,4} | broadcast | bytes 11796480 | tf_op jit(solution)/shard_map/broadcast_in_dim | solution.py:56
  145.3 0.0 copy-start.1
  145.3 0.0 copy-start.4
  145.3 5.2 %all-to-all-start.1 = ((bf16[8,256,3,768]{3,1,2,0:T(8,128)(2,1)}), bf16[8,256,3,768]{3,1,2,0:T(8,128)(2,1)}, u32[]{:S(2)}, u32[]{:S(2)}) async-start(bf16[8,256,3,768]{3,1,2,0:T(8,128)(2,1)} %bitcast.92), calls=%async_computation.1 | async-start | bytes 18874368 | tf_op jit(solution)/shard_map/all_to_all | solution.py:73
  150.5 0.0 copy-done.1
  150.5 0.2 fusion.15
  150.7 0.0 copy-done.4
  150.7 0.2 fusion.17
  150.9 0.0 copy-start.3
  150.9 0.4 collective-permute-start
  151.3 104.4 %all-to-all-done.1 = bf16[8,256,3,768]{3,1,2,0:T(8,128)(2,1)} async-done(((bf16[8,256,3,768]{3,1,2,0:T(8,128)(2,1)}), bf16[8,256,3,768]{3,1,2,0:T(8,128)(2,1)}, u32[]{:S(2)}, u32[]{:S(2)}) %all-to-all-start.1) | async-done | bytes 9437216 | tf_op jit(solution)/shard_map/all_to_all | solution.py:73
  255.8 8.2 %copy.11 = bf16[8,256,3,768]{3,1,0,2:T(8,128)(2,1)} copy(bf16[8,256,3,768]{3,1,2,0:T(8,128)(2,1)} %all-to-all-done.1) | data formatting | bytes 18874368 | tf_op jit(solution)/shard_map/all_to_all | solution.py:73
  264.0 0.0 collective-permute-done
  264.0 0.0 copy-done.3
  264.0 4.6 %fusion.2 = f32[256,2,768]{2,0,1:T(8,128)S(1)} fusion(bf16[2048,3,768]{2,0,1:T(8,128)(2,1)} %bitcast.93, bf16[128,2048]{1,0:T(8,128)(2,1)S(1)} %collective-permute-done, bf16[128,2048]{1,0:T(8,128)(2,1)S(1)} %fusion.17), kind=kOutput, calls=%fused_computation.6 | convolution fusion | flops 1612709888 | bytes 8912896 | tf_op jit(solution)/shard_map/td,dkf->tkf/dot_general | solution.py:74
  268.6 0.0 copy-start.7
  268.6 3.5 %fusion.12 = bf16[256,2048]{1,0:T(8,128)(2,1)S(1)} fusion(bf16[2048,3,768]{2,0,1:T(8,128)(2,1)} %bitcast.94, f32[256,2,768]{2,0,1:T(8,128)S(1)} %fusion.2), kind=kOutput, calls=%fused_computation.16 | convolution fusion | flops 807010304 | bytes 5767168 | tf_op jit(solution)/shard_map/tf,df->td/dot_general | solution.py:82
  272.1 0.0 copy-done.7
  272.1 0.0 copy-start.2
  272.1 0.0 copy-start.6
  272.2 0.1 collective-permute-start.1
  272.3 0.0 copy-done
  272.3 0.6 gather_fusion
  272.9 1.3 fusion.63
  274.2 0.0 collective-permute-done.1
  274.2 0.0 copy-done.2
  274.2 0.3 fusion.24
  274.6 0.0 copy-done.6
  274.6 0.2 fusion.21
  274.9 0.5 collective-permute-start.2
  275.4 1.5 collective-permute-done.2
  276.9 3.4 %fusion.45 = (bf16[256,1,768]{2,0,1:T(8,128)(2,1)S(1)}, bf16[256,1,768]{2,0,1:T(8,128)(2,1)S(1)}) fusion(f32[256,2,768]{2,0,1:T(8,128)} %copy-done.7, bf16[2048,3,768]{2,0,1:T(8,128)(2,1)} %bitcast.95, bf16[128,2048]{1,0:T(8,128)(2,1)S(1)} %collective-permute-done.2, bf16[128,2048]{1,0:T(8,128)(2,1)S(1)} %get-tuple-element.14), kind=kOutput, calls=%fused_computation.69 | convolution fusion | flops 809959424 | bytes 6553600 | tf_op jit(solution)/shard_map/td,df->tf/dot_general | solution.py:101
  280.4 4.6 %fusion.9 = bf16[256,2048]{1,0:T(8,128)(2,1)S(1)} fusion(bf16[2048,3,768]{2,0,1:T(8,128)(2,1)} %bitcast.96, bf16[256,1,768]{2,0,1:T(8,128)(2,1)S(1)} %get-tuple-element.11, bf16[256,1,768]{2,0,1:T(8,128)(2,1)S(1)} %get-tuple-element.10), kind=kOutput, calls=%fused_computation.15 | convolution fusion | flops 1611530240 | bytes 8126464 | tf_op jit(solution)/shard_map/tkf,dkf->td/dot_general | solution.py:108
  285.0 0.4 collective-permute-start.3
  285.5 1.5 collective-permute-done.3
  287.0 0.5 fusion.20
  287.6 1.7 fusion.25
  (15 shorter events, 0.2 us)
Async XLA Ops:
  0.6 271.6 %copy-start = (bf16[2048,32]{0,1:T(8,128)(2,1)S(1)}, bf16[2048,32]{0,1:T(8,128)(2,1)}, u32[]{:S(2)}) copy-start(bf16[2048,32]{0,1:T(8,128)(2,1)} %param.11) | copy-start | bytes 393220
  26.0 6.5 %copy-start.5 = (s32[4,2]{0,1:T(2,128)S(1)}, s32[4,2]{0,1:T(2,128)}, u32[]{:S(2)}) copy-start(s32[4,2]{0,1:T(2,128)} %param.14) | copy-start | bytes 100
  26.0 111.2 %all-to-all-start = ((bf16[4,256,3,768]{3,1,2,0:T(8,128)(2,1)}), bf16[4,256,3,768]{3,1,2,0:T(8,128)(2,1)}, u32[]{:S(2)}, u32[]{:S(2)}) async-start(bf16[4,256,3,768]{3,1,2,0:T(8,128)(2,1)} %select_select_fusion), calls=%async_computation | async-start | bytes 9437184 | tf_op jit(solution)/shard_map/all_to_all | solution.py:54
  145.3 5.2 %copy-start.1 = (bf16[128,2048]{1,0:T(8,128)(2,1)S(1)}, bf16[128,2048]{1,0:T(8,128)(2,1)}, u32[]{:S(2)}) copy-start(bf16[128,2048]{1,0:T(8,128)(2,1)} %param.8) | copy-start | bytes 1572868
  145.3 5.4 %copy-start.4 = (f32[2048]{0:T(1024)S(1)}, f32[2048]{0:T(1024)}, u32[]{:S(2)}) copy-start(f32[2048]{0:T(1024)} %param.10) | copy-start | bytes 24580
  145.3 110.5 %all-to-all-start.1 = ((bf16[8,256,3,768]{3,1,2,0:T(8,128)(2,1)}), bf16[8,256,3,768]{3,1,2,0:T(8,128)(2,1)}, u32[]{:S(2)}, u32[]{:S(2)}) async-start(bf16[8,256,3,768]{3,1,2,0:T(8,128)(2,1)} %bitcast.92), calls=%async_computation.1 | async-start | bytes 18874368 | tf_op jit(solution)/shard_map/all_to_all | solution.py:73
  150.9 113.1 %copy-start.3 = (bf16[128,2048]{1,0:T(8,128)(2,1)}, bf16[128,2048]{1,0:T(8,128)(2,1)S(1)}, u32[]{:S(2)}) copy-start(bf16[128,2048]{1,0:T(8,128)(2,1)S(1)} %fusion.17) | copy-start | bytes 1572868
  150.9 113.1 %collective-permute-start = (bf16[128,2048]{1,0:T(8,128)(2,1)S(1)}, bf16[128,2048]{1,0:T(8,128)(2,1)S(1)}, u32[]{:S(2)}, u32[]{:S(2)}) collective-permute-start(bf16[128,2048]{1,0:T(8,128)(2,1)S(1)} %fusion.17), channel_id=1, source_target_pairs={{0,4},{4,0},{8,12},{12,8},{16,20},{20,16},{24,28},{28,24},{1,5},{5... | collective-permute-start | bytes 1572872 | tf_op jit(solution)/shard_map/ppermute | solution.py:12
  268.6 3.5 %copy-start.7 = (f32[256,2,768]{2,0,1:T(8,128)}, f32[256,2,768]{2,0,1:T(8,128)S(1)}, u32[]{:S(2)}) copy-start(f32[256,2,768]{2,0,1:T(8,128)S(1)} %fusion.2) | copy-start | bytes 4718596
  272.1 2.1 copy-start.2
  272.1 2.5 copy-start.6
  272.2 2.0 collective-permute-start.1
  274.9 2.1 collective-permute-start.2
  285.0 2.0 collective-permute-start.3
where the time goes:
time: 290 us; the launch traced here: 289 us
  waiting for transfers between devices  212 us (73%)
  local copies, waits for them, and re-layouts  28.6 us (10%)
  matrix products  18 us (6%)
  other arithmetic  16.6 us (6%)
  starting transfers between devices  13.1 us (5%)
    all_to_all x1, waiting for transfers between devices, body(): lax.all_to_all(outgoing, 'expert', split_axis=0, concat_axis=0, tiled=True)  105 us
    all_to_all x1, waiting for transfers between devices, body(): lax.all_to_all(spread_out, 'dp', split_axis=0, concat_axis=1, tiled=True)[0]  104 us
    all_to_all x1, local copies, waits for them, and re-layouts, body(): lax.all_to_all(spread_out, 'dp', split_axis=0, concat_axis=1, tiled=True)[0]  8.21 us
    another operation x1, other arithmetic, body(): jnp.stack([gate_up_weight[:, :, :width], gate_up_weight[:, :, width:], do...  6.99 us
    gather x1, local copies, waits for them, and re-layouts, body(): jnp.take(owned, local_pick, axis=0)  6.77 us
    all_to_all x1, starting transfers between devices, body(): lax.all_to_all(outgoing, 'expert', split_axis=0, concat_axis=0, tiled=True)  6.45 us
  transfers between devices with their start and end apart: 6, of which 4 were waited for; matrix products, arithmetic and copies ran while one was open for 4% of the time, Pallas kernels for 0%

commit v1 on v0

--- a/solution.py
+++ b/solution.py
@@ -4,6 +4,22 @@
 from jax.sharding import PartitionSpec as P
 
 eps = 1e-05
+
+
+def pairwise_exchange(shard, axis, split, join):
+    ways, here = (lax.axis_size(axis), lax.axis_index(axis))
+    width = shard.shape[split] // ways
+    dims = list(shard.shape)
+    dims[split] = width
+    height = dims[join]
+    dims[join] = height * ways
+    full = jnp.zeros(dims, shard.dtype)
+    for mask in range(ways):
+        part = lax.dynamic_slice_in_dim(shard, (here ^ mask) * width, width, axis=split)
+        if mask:
+            part = lax.ppermute(part, axis, [(d, d ^ mask) for d in range(ways)])
+        full = lax.dynamic_update_slice_in_dim(full, part, (here ^ mask) * height, axis=join)
+    return full
 
 
 def partner(value, axis, stride):
@@ -51,7 +67,7 @@
         jnp.take(owned, local_pick, axis=0),
         jnp.zeros((), jnp.bfloat16),
     )
-    arrived = lax.all_to_all(outgoing, "expert", split_axis=0, concat_axis=0, tiled=True)
+    arrived = pairwise_exchange(outgoing, "expert", 0, 0)
     slot_rows = jnp.take(arrived, listed // held, axis=0)
     spread_out = jnp.broadcast_to(slot_rows[None], (ranks // 2,) + slot_rows.shape).reshape(
         (ranks,) + slot_rows.shape[1:]

time: 290 us -> 287 us (0.990)
  the two profiles are of different devices: /device:TPU:0 before, /device:TPU:17 now
where the time goes in v1:
time: 287 us; the launch traced here: 286 us
  waiting for transfers between devices  203 us (71%)
  local copies, waits for them, and re-layouts  35.9 us (13%)
  matrix products  18 us (6%)
  other arithmetic  14.4 us (5%)
  starting transfers between devices  14 us (5%)
    all_to_all x1, waiting for transfers between devices, body(): lax.all_to_all(spread_out, 'dp', split_axis=0, concat_axis=1, tiled=True)[0]  101 us
    ppermute x3, waiting for transfers between devices, pairwise_exchange(): part = lax.ppermute(part, axis, [(d, d ^ mask) for d in range(ways)])  98.5 us
    all_to_all x1, local copies, waits for them, and re-layouts, body(): lax.all_to_all(spread_out, 'dp', split_axis=0, concat_axis=1, tiled=True)[0]  8.21 us
    another operation x1, other arithmetic, body(): jnp.stack([gate_up_weight[:, :, :width], gate_up_weight[:, :, width:], do...  6.96 us
    all_to_all x1, starting transfers between devices, body(): lax.all_to_all(spread_out, 'dp', split_axis=0, concat_axis=1, tiled=True)[0]  6.88 us
    gather x1, local copies, waits for them, and re-layouts, body(): jnp.take(owned, local_pick, axis=0)  6.76 us
  transfers between devices with their start and end apart: 8, of which 6 were waited for; matrix products, arithmetic and copies ran while one was open for 5% of the time, Pallas kernels for 0%

profile of v1, /device:TPU:17, one launch (start us, length us, event | category | flops | bytes accessed | tf_op | source)
XLA Modules:
  0.0 286.2 jit_solution(1757520037420373830)
XLA Ops:
  0.6 0.0 copy-start
  0.6 0.7 fusion.65
  1.4 0.7 fusion.50
  2.1 5.0 %slice_bitcast_fusion.2 = (bf16[8,256,1,768]{3,1,0,2:T(8,128)(2,1)S(1)}, bf16[8,256,1,768]{3,1,0,2:T(8,128)(2,1)}) fusion(bf16[8,256,1536]{2,1,0:T(8,128)(2,1)} %param.12), kind=kLoop, calls=%fused_computation.11 | loop fusion | bytes 12582912 | tf_op jit(solution)/shard_map/stack | solution.py:62
  7.1 7.0 %pad_maximum_fusion = bf16[8,256,3,768]{3,1,0,2:T(8,128)(2,1)} fusion(bf16[8,256,1,768]{3,1,0,2:T(8,128)(2,1)} %bitcast.97, bf16[8,256,1,768]{3,1,0,2:T(8,128)(2,1)} %get-tuple-element.9, bf16[8,256,1,768]{3,1,0,2:T(8,128)(2,1)S(1)} %get-tuple-element.8), kind=kLoop, calls=%fused_computation.3 | loop fusion | flops 9437184 | bytes 18874368 | tf_op jit(solution)/shard_map/stack | solution.py:62
  14.1 6.8 %gather_fusion.1 = bf16[4,256,3,768]{3,1,2,0:T(8,128)(2,1)} fusion(bf16[8,256,3,768]{3,1,0,2:T(8,128)(2,1)} %pad_maximum_fusion, s32[1024]{0:T(1024)S(1)} %pad_clamp_fusion.1), kind=kCustom, calls=%fused_computation.1 | custom fusion | bytes 9437200 | tf_op jit(solution)/shard_map/jit(_take)/gather | solution.py:67
  20.9 2.9 %select_select_fusion = bf16[4,256,3,768]{3,1,2,0:T(8,128)(2,1)S(1)} fusion(bf16[4,256,3,768]{3,1,2,0:T(8,128)(2,1)} %gather_fusion.1, pred[4]{0:T(512)(128)(4,1)S(1)} %compare_and_fusion, pred[4]{0:T(512)(128)(4,1)S(1)} %get-tuple-element.6), kind=kLoop, calls=%fused_computation.8 | loop fusion | flops 4718592 | bytes 9437192 | tf_op jit(solution)/shard_map/jit(_where)/select_n | solution.py:65
  23.8 2.5 broadcast_in_dim.65
  26.3 0.0 copy-start.5
  26.3 1.4 constant_dynamic-slice_fusion.1
  27.7 1.3 collective-permute-start.1
  29.0 0.1 collective-permute-start.2
  29.0 1.3 collective-permute-start.3
  30.3 0.0 copy-done.5
  30.3 0.2 fusion.47
  30.6 47.0 %collective-permute-done.1 = bf16[1,256,3,768]{3,1,2,0:T(8,128)(2,1)S(1)} collective-permute-done((bf16[1,256,3,768]{3,1,2,0:T(8,128)(2,1)S(1)}, bf16[1,256,3,768]{3,1,2,0:T(8,128)(2,1)S(1)}, u32[]{:S(2)}, u32[]{:S(2)}) %collective-permute-start.1) | collective-permute-done | bytes 1179680 | tf_op jit(solution)/shard_map/ppermute | solution.py:20
  77.6 1.1 constant_dynamic-update-slice_fusion.2
  78.7 1.1 collective-permute-done.2
  79.7 1.1 constant_dynamic-update-slice_fusion.1
  80.8 50.5 %collective-permute-done.3 = bf16[1,256,3,768]{3,1,2,0:T(8,128)(2,1)S(1)} collective-permute-done((bf16[1,256,3,768]{3,1,2,0:T(8,128)(2,1)S(1)}, bf16[1,256,3,768]{3,1,2,0:T(8,128)(2,1)S(1)}, u32[]{:S(2)}, u32[]{:S(2)}) %collective-permute-start.3) | collective-permute-done | bytes 1179680 | tf_op jit(solution)/shard_map/ppermute | solution.py:20
  131.3 1.1 constant_dynamic-update-slice_fusion
  132.4 3.0 %gather_fusion.2 = bf16[2,256,3,768]{3,1,2,0:T(8,128)(2,1)S(1)} fusion(bf16[4,256,3,768]{3,1,2,0:T(8,128)(2,1)} %constant_dynamic-update-slice_fusion, s32[1024]{0:T(1024)S(1)} %pad_clamp_fusion), kind=kCustom, calls=%fused_computation.2 | custom fusion | bytes 4718600 | tf_op jit(solution)/shard_map/jit(_take)/gather | solution.py:71
  135.4 0.3 broadcast_select_fusion
  135.7 4.7 %broadcast_in_dim.70 = bf16[4,2,256,3,768]{4,2,3,1,0:T(8,128)(2,1)} broadcast(bf16[2,256,3,768]{3,1,2,0:T(8,128)(2,1)S(1)} %broadcast_select_fusion), dimensions={1,2,3,4} | broadcast | bytes 11796480 | tf_op jit(solution)/shard_map/broadcast_in_dim | solution.py:72
  140.5 0.0 copy-start.1
  140.5 0.0 copy-start.4
  140.5 6.9 %all-to-all-start = ((bf16[8,256,3,768]{3,1,2,0:T(8,128)(2,1)}), bf16[8,256,3,768]{3,1,2,0:T(8,128)(2,1)}, u32[]{:S(2)}, u32[]{:S(2)}) async-start(bf16[8,256,3,768]{3,1,2,0:T(8,128)(2,1)} %bitcast.92), calls=%async_computation | async-start | bytes 18874368 | tf_op jit(solution)/shard_map/all_to_all | solution.py:89
  147.4 0.0 copy-done.1
  147.4 0.2 fusion.15
  147.6 0.0 copy-done.4
  147.6 0.2 fusion.17
  147.8 0.0 copy-start.3
  147.8 0.4 collective-permute-start
  148.2 100.9 %all-to-all-done = bf16[8,256,3,768]{3,1,2,0:T(8,128)(2,1)} async-done(((bf16[8,256,3,768]{3,1,2,0:T(8,128)(2,1)}), bf16[8,256,3,768]{3,1,2,0:T(8,128)(2,1)}, u32[]{:S(2)}, u32[]{:S(2)}) %all-to-all-start) | async-done | bytes 9437216 | tf_op jit(solution)/shard_map/all_to_all | solution.py:89
  249.1 8.2 %copy.11 = bf16[8,256,3,768]{3,1,0,2:T(8,128)(2,1)} copy(bf16[8,256,3,768]{3,1,2,0:T(8,128)(2,1)} %all-to-all-done) | data formatting | bytes 18874368 | tf_op jit(solution)/shard_map/all_to_all | solution.py:89
  257.3 0.0 collective-permute-done
  257.3 0.0 copy-done.3
  257.3 4.6 %fusion.2 = f32[256,2,768]{2,0,1:T(8,128)S(1)} fusion(bf16[2048,3,768]{2,0,1:T(8,128)(2,1)} %bitcast.93, bf16[128,2048]{1,0:T(8,128)(2,1)S(1)} %collective-permute-done, bf16[128,2048]{1,0:T(8,128)(2,1)S(1)} %fusion.17), kind=kOutput, calls=%fused_computation.6 | convolution fusion | flops 1612709888 | bytes 8912896 | tf_op jit(solution)/shard_map/td,dkf->tkf/dot_general | solution.py:90
  261.9 0.0 copy-start.7
  261.9 3.5 %fusion.12 = bf16[256,2048]{1,0:T(8,128)(2,1)S(1)} fusion(bf16[2048,3,768]{2,0,1:T(8,128)(2,1)} %bitcast.94, f32[256,2,768]{2,0,1:T(8,128)S(1)} %fusion.2), kind=kOutput, calls=%fused_computation.16 | convolution fusion | flops 807010304 | bytes 5767168 | tf_op jit(solution)/shard_map/tf,df->td/dot_general | solution.py:98
  265.4 0.0 copy-done.7
  265.4 0.0 copy-start.2
  265.4 0.0 copy-start.6
  265.5 3.8 %collective-permute-start.4 = (bf16[128,2048]{1,0:T(8,128)(2,1)S(1)}, bf16[128,2048]{1,0:T(8,128)(2,1)S(1)}, u32[]{:S(2)}, u32[]{:S(2)}) collective-permute-start(bf16[128,2048]{1,0:T(8,128)(2,1)S(1)} %slice.53), channel_id=1, source_target_pairs={{0,4},{4,0},{8,12},{12,8},{16,20},{20,16},{24,28},{28,24},{1,5},{5... | collective-permute-start | bytes 1572872 | tf_op jit(solution)/shard_map/ppermute | solution.py:28
  269.3 0.0 copy-done
  269.3 0.6 gather_fusion
  269.8 1.3 fusion.64
  271.2 0.0 collective-permute-done.4
  271.2 0.0 copy-done.2
  271.2 0.3 fusion.24
  271.5 0.0 copy-done.6
  271.6 0.2 fusion.21
  271.8 0.1 collective-permute-start.5
  271.9 1.9 collective-permute-done.5
  273.8 3.4 %fusion.45 = (bf16[256,1,768]{2,0,1:T(8,128)(2,1)S(1)}, bf16[256,1,768]{2,0,1:T(8,128)(2,1)S(1)}) fusion(f32[256,2,768]{2,0,1:T(8,128)} %copy-done.7, bf16[2048,3,768]{2,0,1:T(8,128)(2,1)} %bitcast.95, bf16[128,2048]{1,0:T(8,128)(2,1)S(1)} %collective-permute-done.5, bf16[128,2048]{1,0:T(8,128)(2,1)S(1)} %get-tuple-element.18), kind=kOutput, calls=%fused_computation.70 | convolution fusion | flops 809959424 | bytes 6553600 | tf_op jit(solution)/shard_map/td,df->tf/dot_general | solution.py:117
  277.3 4.6 %fusion.9 = bf16[256,2048]{1,0:T(8,128)(2,1)S(1)} fusion(bf16[2048,3,768]{2,0,1:T(8,128)(2,1)} %bitcast.96, bf16[256,1,768]{2,0,1:T(8,128)(2,1)S(1)} %get-tuple-element.15, bf16[256,1,768]{2,0,1:T(8,128)(2,1)S(1)} %get-tuple-element.14), kind=kOutput, calls=%fused_computation.15 | convolution fusion | flops 1611530240 | bytes 8126464 | tf_op jit(solution)/shard_map/tkf,dkf->td/dot_general | solution.py:124
  281.9 0.2 collective-permute-start.6
  282.1 1.8 collective-permute-done.6
  283.9 0.5 fusion.20
  284.5 1.7 fusion.25
  (15 shorter events, 0.2 us)
Async XLA Ops:
  0.6 268.6 %copy-start = (bf16[2048,32]{0,1:T(8,128)(2,1)S(1)}, bf16[2048,32]{0,1:T(8,128)(2,1)}, u32[]{:S(2)}) copy-start(bf16[2048,32]{0,1:T(8,128)(2,1)} %param.11) | copy-start | bytes 393220
  26.3 4.0 %copy-start.5 = (s32[4,2]{0,1:T(2,128)S(1)}, s32[4,2]{0,1:T(2,128)}, u32[]{:S(2)}) copy-start(s32[4,2]{0,1:T(2,128)} %param.14) | copy-start | bytes 100
  27.7 49.9 %collective-permute-start.1 = (bf16[1,256,3,768]{3,1,2,0:T(8,128)(2,1)S(1)}, bf16[1,256,3,768]{3,1,2,0:T(8,128)(2,1)S(1)}, u32[]{:S(2)}, u32[]{:S(2)}) collective-permute-start(bf16[1,256,3,768]{3,1,2,0:T(8,128)(2,1)S(1)} %get-tuple-element.12), channel_id=1, source_target_pairs={{0,1},{1,0},{2,3},{3,2},{4,5},{5,4},{6,7},{7,6},{8,9},{9,8},{10,11... | collective-permute-start | bytes 3538952 | tf_op jit(solution)/shard_map/ppermute | solution.py:20
  29.0 50.7 %collective-permute-start.2 = (bf16[1,256,3,768]{3,1,2,0:T(8,128)(2,1)S(1)}, bf16[1,256,3,768]{3,1,2,0:T(8,128)(2,1)S(1)}, u32[]{:S(2)}, u32[]{:S(2)}) collective-permute-start(bf16[1,256,3,768]{3,1,2,0:T(8,128)(2,1)S(1)} %get-tuple-element.11), channel_id=1, source_target_pairs={{0,2},{1,3},{2,0},{3,1},{4,6},{5,7},{6,4},{7,5},{8,10},{9,11},{10,... | collective-permute-start | bytes 3538952 | tf_op jit(solution)/shard_map/ppermute | solution.py:20
  29.0 102.3 %collective-permute-start.3 = (bf16[1,256,3,768]{3,1,2,0:T(8,128)(2,1)S(1)}, bf16[1,256,3,768]{3,1,2,0:T(8,128)(2,1)S(1)}, u32[]{:S(2)}, u32[]{:S(2)}) collective-permute-start(bf16[1,256,3,768]{3,1,2,0:T(8,128)(2,1)S(1)} %get-tuple-element.10), channel_id=1, source_target_pairs={{0,3},{1,2},{2,1},{3,0},{4,7},{5,6},{6,5},{7,4},{8,11},{9,10},{10,... | collective-permute-start | bytes 3538952 | tf_op jit(solution)/shard_map/ppermute | solution.py:20
  140.5 6.9 %copy-start.1 = (bf16[128,2048]{1,0:T(8,128)(2,1)S(1)}, bf16[128,2048]{1,0:T(8,128)(2,1)}, u32[]{:S(2)}) copy-start(bf16[128,2048]{1,0:T(8,128)(2,1)} %param.8) | copy-start | bytes 1572868
  140.5 7.1 %copy-start.4 = (f32[2048]{0:T(1024)S(1)}, f32[2048]{0:T(1024)}, u32[]{:S(2)}) copy-start(f32[2048]{0:T(1024)} %param.10) | copy-start | bytes 24580
  140.5 108.6 %all-to-all-start = ((bf16[8,256,3,768]{3,1,2,0:T(8,128)(2,1)}), bf16[8,256,3,768]{3,1,2,0:T(8,128)(2,1)}, u32[]{:S(2)}, u32[]{:S(2)}) async-start(bf16[8,256,3,768]{3,1,2,0:T(8,128)(2,1)} %bitcast.92), calls=%async_computation | async-start | bytes 18874368 | tf_op jit(solution)/shard_map/all_to_all | solution.py:89
  147.8 109.5 %copy-start.3 = (bf16[128,2048]{1,0:T(8,128)(2,1)}, bf16[128,2048]{1,0:T(8,128)(2,1)S(1)}, u32[]{:S(2)}) copy-start(bf16[128,2048]{1,0:T(8,128)(2,1)S(1)} %fusion.17) | copy-start | bytes 1572868
  147.8 109.5 %collective-permute-start = (bf16[128,2048]{1,0:T(8,128)(2,1)S(1)}, bf16[128,2048]{1,0:T(8,128)(2,1)S(1)}, u32[]{:S(2)}, u32[]{:S(2)}) collective-permute-start(bf16[128,2048]{1,0:T(8,128)(2,1)S(1)} %fusion.17), channel_id=1, source_target_pairs={{0,4},{4,0},{8,12},{12,8},{16,20},{20,16},{24,28},{28,24},{1,5},{5... | collective-permute-start | bytes 1572872 | tf_op jit(solution)/shard_map/ppermute | solution.py:28
  261.9 3.5 %copy-start.7 = (f32[256,2,768]{2,0,1:T(8,128)}, f32[256,2,768]{2,0,1:T(8,128)S(1)}, u32[]{:S(2)}) copy-start(f32[256,2,768]{2,0,1:T(8,128)S(1)} %fusion.2) | copy-start | bytes 4718596
  265.4 5.8 %copy-start.2 = (bf16[128,2048]{1,0:T(8,128)(2,1)S(1)}, bf16[128,2048]{1,0:T(8,128)(2,1)}, u32[]{:S(2)}) copy-start(bf16[128,2048]{1,0:T(8,128)(2,1)} %param.9) | copy-start | bytes 1572868
  265.4 6.2 %copy-start.6 = (s32[128,1]{0,1:T(1,128)S(1)}, s32[128,1]{0,1:T(1,128)}, u32[]{:S(2)}) copy-start(s32[128,1]{0,1:T(1,128)} %param.15) | copy-start | bytes 1540
  265.5 5.7 %collective-permute-start.4 = (bf16[128,2048]{1,0:T(8,128)(2,1)S(1)}, bf16[128,2048]{1,0:T(8,128)(2,1)S(1)}, u32[]{:S(2)}, u32[]{:S(2)}) collective-permute-start(bf16[128,2048]{1,0:T(8,128)(2,1)S(1)} %slice.53), channel_id=1, source_target_pairs={{0,4},{4,0},{8,12},{12,8},{16,20},{20,16},{24,28},{28,24},{1,5},{5... | collective-permute-start | bytes 1572872 | tf_op jit(solution)/shard_map/ppermute | solution.py:28
  271.8 2.0 collective-permute-start.5
  281.9 2.0 collective-permute-start.6
